TPU v7x, 32 devices: a whole 2x2x4 slice. The times are simulated.
32 devices in a mesh: seg: 2 (over core), dp: 16 (over z, y, x).
Axes of the slice: x: 2, y: 2, z: 4, core: 2. Of those that a mesh axis runs over, the one named last changes fastest.
Arguments:
- query_rows: bfloat16 [16, 1024, 1280], P('dp', 'seg'), may hold values from -160 to 160
- key_rows: bfloat16 [16, 1024, 1280], P('dp', 'seg'), may hold values from -8 to 8
- value_rows: bfloat16 [16, 1024, 1280], P('dp', 'seg'), may hold values from -6 to 6
- prompt_keys: bfloat16 [16, 100, 1280], P('dp', 'seg'), may hold values from -6 to 6
- prompt_values: bfloat16 [16, 100, 1280], P('dp', 'seg'), may hold values from -6 to 6
- out_grad: bfloat16 [16, 1024, 2560], P('dp', 'seg'), may hold values from -54 to 54
- w_out: bfloat16 [1280, 2560], replicated, may hold values from -0.15625 to 0.15625
Outputs:
- query_grad: bfloat16 [16, 1024, 1280], P('dp', 'seg')
- key_grad: bfloat16 [16, 1024, 1280], P('dp', 'seg')
- value_grad: bfloat16 [16, 1024, 1280], P('dp', 'seg')
- prompt_key_grad: bfloat16 [16, 100, 1280], P('dp', 'seg')
- prompt_value_grad: bfloat16 [16, 100, 1280], P('dp', 'seg')
- weight_grad: bfloat16 [1280, 2560], replicated
All inputs are finite; a program needn't handle non-finite values.
Results may differ from a plain program's by a relative error of at most 0.0058.
Values may be sent and summed in bfloat16 or wider, within the bound.
A program may use at most 256 MiB of HBM per device.

v0:
```python
import jax
import jax.numpy as jnp
from jax import lax
from jax.sharding import PartitionSpec as P

HEADS = 16
SUMS = 50


def prefix_2(shard, axis, combine, identity):
    devices, mine = (lax.axis_size(axis), lax.axis_index(axis))
    everything = jax.tree.map(
        lambda part, kind: lax.all_gather(part.astype(kind), axis),
        shard,
        (jnp.bfloat16, jnp.bfloat16),
    )
    start = jax.tree.map(
        lambda part, zero: jnp.broadcast_to(jnp.asarray(zero, part.dtype), part.shape),
        shard,
        identity,
    )

    def step(k, before):
        at = devices - 1 - k
        reached = at > mine
        new = combine(
            before, jax.tree.map(lambda part, own: part[at].astype(own.dtype), everything, shard)
        )
        return jax.tree.map(lambda a, b: jnp.where(reached, a, b), new, before)

    return lax.fori_loop(0, devices, step, start)


def attend_back(query_seg, key_seg, value_seg, prompt_k, prompt_v, head_low, segment):
    tokens_dev = query_seg.shape[0]
    head_size = query_seg.shape[1] // HEADS
    scaling = head_size ** (-0.5)
    prefix = prompt_k.shape[0]
    keys_all = jnp.concatenate([prompt_k, key_seg], 0).reshape(-1, HEADS, head_size)
    values_all = jnp.concatenate([prompt_v, value_seg], 0).reshape(-1, HEADS, head_size)
    query_heads = query_seg.reshape(tokens_dev, HEADS, head_size)
    grad_heads = head_low.reshape(tokens_dev, HEADS, head_size)
    scores = (
        jnp.einsum("qhd,khd->hqk", query_heads, keys_all, preferred_element_type=jnp.float32)
        * scaling
    )
    row_ids = jnp.arange(tokens_dev, dtype=jnp.int32)
    col_ids = jnp.arange(prefix + tokens_dev, dtype=jnp.int32)
    visible = jnp.where(
        col_ids[None, :] < prefix,
        (col_ids // SUMS < segment)[None, :],
        (col_ids - prefix)[None, :] <= row_ids[:, None],
    )
    scores = jnp.where(visible[None], scores, jnp.float32(-1e30))
    row_max = jnp.max(scores, -1, keepdims=True)
    weights = jnp.exp(scores - row_max)
    probs = weights / jnp.sum(weights, -1, keepdims=True)
    probs_low = probs.astype(jnp.bfloat16)
    attn = (
        jnp.einsum("hqk,khd->qhd", probs_low, values_all, preferred_element_type=jnp.float32)
        .reshape(tokens_dev, -1)
        .astype(jnp.bfloat16)
    )
    prob_grad = jnp.einsum(
        "qhd,khd->hqk", grad_heads, values_all, preferred_element_type=jnp.float32
    )
    row_delta = jnp.sum(probs * prob_grad, -1, keepdims=True)
    score_grad = (scaling * probs * (prob_grad - row_delta)).astype(jnp.bfloat16)
    query_grad = (
        jnp.einsum("hqk,khd->qhd", score_grad, keys_all, preferred_element_type=jnp.float32)
        .reshape(tokens_dev, -1)
        .astype(jnp.bfloat16)
    )
    key_all_grad = jnp.einsum(
        "hqk,qhd->khd", score_grad, query_heads, preferred_element_type=jnp.float32
    ).reshape(prefix + tokens_dev, -1)
    value_all_grad = jnp.einsum(
        "hqk,qhd->khd", probs_low, grad_heads, preferred_element_type=jnp.float32
    ).reshape(prefix + tokens_dev, -1)
    return (
        query_grad,
        key_all_grad[prefix:].astype(jnp.bfloat16),
        value_all_grad[prefix:].astype(jnp.bfloat16),
        key_all_grad[:prefix],
        value_all_grad[:prefix],
        attn,
    )


def add_pair(earlier, later):
    return (earlier[0] + later[0], earlier[1] + later[1])


def shards(query_rows, key_rows, value_rows, prompt_keys, prompt_values, out_grad, w_out):
    segment = lax.axis_index("seg")
    grad_rows = out_grad[0]
    prompt_k, prompt_v = (
        lax.all_gather(prompt_keys[0], "seg", axis=0, tiled=True),
        lax.all_gather(prompt_values[0], "seg", axis=0, tiled=True),
    )
    head_low = jnp.einsum("td,hd->th", grad_rows, w_out, preferred_element_type=jnp.float32).astype(
        jnp.bfloat16
    )
    outputs = attend_back(
        query_rows[0], key_rows[0], value_rows[0], prompt_k, prompt_v, head_low, segment
    )
    query_grad, key_grad, value_grad, pk_part, pv_part, attn = outputs
    weight_part = jnp.einsum("th,td->hd", attn, grad_rows, preferred_element_type=jnp.float32)
    weight_total = lax.psum(weight_part, ("seg", "dp"))
    rms_value = jnp.sqrt(jnp.mean(weight_total * weight_total) + 1e-06)
    weight_grad = (weight_total * jnp.minimum(1.0, 1.0 / rms_value)).astype(jnp.bfloat16)
    empty = jnp.zeros_like(pk_part)
    later_k, later_v = prefix_2((pk_part, pv_part), "seg", add_pair, (empty, empty))
    start = segment * SUMS
    own_k = lax.dynamic_slice_in_dim(later_k, start, SUMS, 0)
    own_v = lax.dynamic_slice_in_dim(later_v, start, SUMS, 0)
    return (
        query_grad[None],
        key_grad[None],
        value_grad[None],
        own_k.astype(jnp.bfloat16)[None],
        own_v.astype(jnp.bfloat16)[None],
        weight_grad,
    )


def solution(mesh):
    placed = (
        P("dp", "seg", None),
        P("dp", "seg", None),
        P("dp", "seg", None),
        P("dp", "seg", None),
        P("dp", "seg", None),
        P("dp", "seg", None),
        P(),
    )
    return jax.shard_map(
        shards,
        mesh=mesh,
        in_specs=placed,
        out_specs=(
            P("dp", "seg", None),
            P("dp", "seg", None),
            P("dp", "seg", None),
            P("dp", "seg", None),
            P("dp", "seg", None),
            P(),
        ),
        check_vma=False,
    )
```

profile of v0, /device:TPU:0, one launch (start us, length us, event | category | flops | bytes accessed | tf_op | source)
XLA Modules:
  0.0 338.0 jit_solution(6164413302617033889)
XLA Ops:
  7.2 0.0 copy-start
  7.2 0.0 copy-start.8
  7.2 0.0 all-reduce.2.cloned.1.call-start
  7.3 2.6 copy.39
  9.9 2.4 copy.40
  12.3 0.2 copy.37
  12.5 2.3 all-gather
  14.7 0.5 copy.38
  15.2 2.4 copy.44
  17.7 1.1 copy.42
  18.8 2.2 all-gather.1
  21.0 1.1 copy.43
  22.1 1.0 fusion.22
  23.1 13.4 %fusion.24 = f32[16,612,512]{2,1,0:T(8,128)} fusion(bf16[512,16,80]{0,2,1:T(8,128)(2,1)} %bitcast.58, bf16[512,16,80]{0,2,1:T(8,128)(2,1)} %bitcast.56, bf16[100,16,80]{0,2,1:T(8,128)(2,1)S(1)} %bitcast.63), kind=kOutput, calls=%fused_computation.33 | convolution fusion | flops 805294080 | bytes 22931456 | tf_op jit(solution)/shard_map/qhd,khd->hqk/dot_general | solution.py:44
  36.5 21.7 %fusion.37 = (f32[16,512]{1,0:T(8,128)S(1)}, f32[16,512,612]{1,2,0:T(8,128)}) fusion(f32[16,612,512]{2,1,0:T(8,128)} %fusion.24, pred[512,612]{0,1:T(8,128)(4,1)} %fusion.22), kind=kOutput, calls=%fused_computation.54 | output fusion | flops 30081636 | bytes 40454144 | tf_op jit(solution)/shard_map/sub | solution.py:56
  58.2 9.4 %fusion.15 = bf16[16,80,512]{2,1,0:T(8,128)(2,1)S(1)} fusion(bf16[512,16,80]{0,2,1:T(8,128)(2,1)} %bitcast.65, bf16[100,16,80]{0,2,1:T(8,128)(2,1)S(1)} %bitcast.71, f32[16,512,612]{1,2,0:T(8,128)} %get-tuple-element.217, f32[16,512]{1,0:T(8,128)S(1)} %get-tuple-element.216), kind=kOutput, calls=%fused_computation.26 | convolution fusion | flops 815976448 | bytes 22964224 | tf_op jit(solution)/shard_map/hqk,khd->qhd/dot_general | solution.py:60
  67.6 6.6 %fusion.9 = f32[1280,2560]{1,0:T(8,128)} fusion(bf16[512,1280]{0,1:T(8,128)(2,1)S(1)} %bitcast.73, bf16[1,512,2560]{2,1,0:T(8,128)(2,1)S(1)} %copy-done), kind=kOutput, calls=%fused_computation.19 | convolution fusion | flops 3355443200 | bytes 17039360 | tf_op jit(solution)/shard_map/th,td->hd/dot_general | solution.py:108
  74.2 0.0 all-reduce.2.cloned.1.call-update
  74.2 7.5 %convolution_convert_fusion = bf16[512,1280]{1,0:T(8,128)(2,1)} fusion(bf16[1280,2560]{1,0:T(8,128)(2,1)} %param.15, bf16[1,512,2560]{2,1,0:T(8,128)(2,1)S(1)} %copy-done), kind=kOutput, calls=%fused_computation.18 | convolution fusion | flops 3356098560 | bytes 10485760 | tf_op jit(solution)/shard_map/td,hd->th/dot_general | solution.py:101
  81.7 1.9 copy.41
  83.7 0.0 copy-start.5
  83.7 14.3 %multiply_reduce_fusion = (f32[16,512]{1,0:T(8,128)S(1)}, f32[16,512,612]{1,2,0:T(8,128)}) fusion(f32[16,512,612]{1,2,0:T(8,128)} %get-tuple-element.217, f32[16,512]{1,0:T(8,128)S(1)} %get-tuple-element.216, bf16[512,16,80]{0,2,1:T(8,128)(2,1)S(1)} %bitcast.67, bf16[512,16,80]{0,2,1:T(8,128)(2,1)} %bitcast.66, bf16[100,16,80]{0,2,1:T(8,128)(2,1)S(1)} %bitcast.72), kind=kOutput, calls=%fused_computation.5 | convolution fusion | flops 820326400 | bytes 43051008 | tf_op jit(solution)/shard_map/qhd,khd->hqk/dot_general | solution.py:64
  98.0 18.8 %multiply_convert_fusion = bf16[16,512,612]{1,2,0:T(8,128)(2,1)} fusion(f32[16,512,612]{1,2,0:T(8,128)} %get-tuple-element.219, f32[16,512]{1,0:T(8,128)S(1)} %get-tuple-element.218, f32[16,512,612]{1,2,0:T(8,128)} %get-tuple-element.217, f32[16,512]{1,0:T(8,128)S(1)} %get-tuple-element.216), kind=kLoop, calls=%fused_computation.4 | loop fusion | flops 25067520 | bytes 50200576 | tf_op jit(solution)/shard_map/convert_element_type | solution.py:68
  116.9 0.0 copy-done.3
  116.9 7.6 %fusion.21 = bf16[612,16,80]{0,2,1:T(8,128)(2,1)S(1)} fusion(bf16[16,512,612]{1,2,0:T(8,128)(2,1)} %multiply_convert_fusion, bf16[512,16,80]{0,2,1:T(8,128)(2,1)S(1)} %bitcast.59), kind=kOutput, calls=%fused_computation.29 | convolution fusion | flops 802944000 | bytes 12904448 | tf_op jit(solution)/shard_map/hqk,qhd->khd/dot_general | solution.py:74
  124.5 0.1 slice.26
  124.5 1.6 slice.24
  126.2 10.3 %fusion.18 = bf16[612,16,80]{0,2,1:T(8,128)(2,1)S(1)} fusion(bf16[512,16,80]{0,2,1:T(8,128)(2,1)S(1)} %bitcast.68, f32[16,512,612]{1,2,0:T(8,128)} %get-tuple-element.217, f32[16,512]{1,0:T(8,128)S(1)} %get-tuple-element.216), kind=kOutput, calls=%fused_computation.28 | convolution fusion | flops 812971008 | bytes 22964224 | tf_op jit(solution)/shard_map/hqk,qhd->khd/dot_general | solution.py:77
  136.5 0.8 slice.27
  137.3 1.7 slice.25
  139.0 0.2 copy.45
  139.2 1.2 copy.46
  140.3 2.4 copy.48
  142.8 0.0 copy-done.2
  142.8 7.2 %convolution_convert_fusion.2 = bf16[16,80,512]{2,1,0:T(8,128)(2,1)} fusion(bf16[16,512,612]{1,2,0:T(8,128)(2,1)} %multiply_convert_fusion, bf16[512,16,80]{0,2,1:T(8,128)(2,1)S(1)} %bitcast.57, bf16[100,16,80]{0,2,1:T(8,128)(2,1)S(1)} %bitcast.64), kind=kOutput, calls=%fused_computation.27 | convolution fusion | flops 805949440 | bytes 12904448 | tf_op jit(solution)/shard_map/hqk,khd->qhd/dot_general | solution.py:70
  150.0 2.5 copy.47
  152.5 1.4 copy.49
  154.0 2.2 all_gather.16
  156.2 2.2 all_gather.17
  158.3 0.8 while.18
  158.3 0.4 add_select_fusion.4
  158.7 0.4 add_select_fusion.4
  159.1 0.7 fusion.26
  159.8 0.7 fusion.25
  160.5 151.9 %all-reduce.2.cloned.1.call-done = f32[1280,2560]{1,0:T(8,128)} async-done(((f32[1280,2560]{1,0:T(8,128)}), f32[1280,2560]{1,0:T(8,128)}) %all-reduce.2.cloned.1.call-update) | async-done | bytes 13107216 | tf_op jit(solution)/shard_map/psum | solution.py:109
  312.4 8.7 %multiply_reduce_fusion.1 = f32[]{:T(128)} fusion(f32[1280,2560]{1,0:T(8,128)} %all-reduce.2.cloned.1.call-done), kind=kLoop, calls=%fused_computation.9 | loop fusion | flops 6553599 | bytes 13107204 | tf_op jit(solution)/shard_map/reduce_sum | solution.py:110
  321.8 0.0 copy-start.1
  321.8 9.3 %multiply_convert_fusion.1 = bf16[1280,2560]{1,0:T(8,128)(2,1)} fusion(f32[1280,2560]{1,0:T(8,128)} %all-reduce.2.cloned.1.call-done, f32[]{:T(128)S(6)} %min.3), kind=kLoop, calls=%fused_computation.8 | loop fusion | flops 6553600 | bytes 19660804 | tf_op jit(solution)/shard_map/convert_element_type | solution.py:111
  (16 shorter events, 0.0 us)
Async XLA Ops:
  7.2 60.4 %copy-start = (bf16[1,512,2560]{2,1,0:T(8,128)(2,1)S(1)}, bf16[1,512,2560]{2,1,0:T(8,128)(2,1)}, u32[]{:S(2)}) copy-start(bf16[1,512,2560]{2,1,0:T(8,128)(2,1)} %param.14) | copy-start | bytes 7864324
  7.2 5.1 %copy-start.8 = (bf16[1,50,1280]{2,1,0:T(8,128)(2,1)S(1)}, bf16[1,50,1280]{2,1,0:T(8,128)(2,1)}, u32[]{:S(2)}) copy-start(bf16[1,50,1280]{2,1,0:T(8,128)(2,1)} %param.12) | copy-start | bytes 384004
  7.2 305.2 %all-reduce.2.cloned.1.call-start = ((), (), s32[]{:S(2)}) async-start(), calls=%async_computation | async-start | bytes 26214400 | tf_op jit(solution)/shard_map/psum | solution.py:109
  36.5 21.7 %copy-start.7 = (bf16[1,100,1280]{1,2,0:T(8,128)(2,1)S(1)}, bf16[1,100,1280]{1,2,0:T(8,128)(2,1)}, u32[]{:S(2)}) copy-start(bf16[1,100,1280]{1,2,0:T(8,128)(2,1)} %copy.43) | copy-start | bytes 768004
  83.7 14.4 %copy-start.5 = (bf16[512,1280]{0,1:T(8,128)(2,1)}, bf16[512,1280]{0,1:T(8,128)(2,1)S(1)}, u32[]{:S(2)}) copy-start(bf16[512,1280]{0,1:T(8,128)(2,1)S(1)} %copy.41) | copy-start | bytes 3932164
  98.0 18.8 %copy-start.3 = (bf16[1,512,1280]{1,2,0:T(8,128)(2,1)S(1)}, bf16[1,512,1280]{1,2,0:T(8,128)(2,1)}, u32[]{:S(2)}) copy-start(bf16[1,512,1280]{1,2,0:T(8,128)(2,1)} %copy.40) | copy-start | bytes 3932164
  116.9 9.3 %copy-start.6 = (bf16[512,1280]{0,1:T(8,128)(2,1)S(1)}, bf16[512,1280]{0,1:T(8,128)(2,1)}, u32[]{:S(2)}) copy-start(bf16[512,1280]{0,1:T(8,128)(2,1)} %copy-done.5) | copy-start | bytes 3932164
  137.3 5.5 %copy-start.2 = (bf16[1,512,1280]{1,2,0:T(8,128)(2,1)S(1)}, bf16[1,512,1280]{1,2,0:T(8,128)(2,1)}, u32[]{:S(2)}) copy-start(bf16[1,512,1280]{1,2,0:T(8,128)(2,1)} %copy.39) | copy-start | bytes 3932164
  150.0 2.5 copy-start.4
  321.8 9.3 %copy-start.1 = (bf16[1,512,2560]{2,1,0:T(8,128)(2,1)S(1)}, bf16[1,512,2560]{2,1,0:T(8,128)(2,1)}, u32[]{:S(2)}) copy-start(bf16[1,512,2560]{2,1,0:T(8,128)(2,1)} %param.14) | copy-start | bytes 7864324
Sparse Core Ops, SparseCore 0:
  74.4 238.0 all-reduce.1
where the time goes:
time: 339 us; the launch traced here: 338 us
  waiting for transfers between devices  152 us (45%)
  matrix products  76.4 us (23%)
  other arithmetic  60.3 us (18%)
  local copies, waits for them, and re-layouts  25.6 us (8%)
  between operations  14.9 us (4%)
  blocking collectives  8.77 us (3%)
    psum x1, waiting for transfers between devices, shards(): weight_total = lax.psum(weight_part, ('seg', 'dp'))  152 us
    sub x1, other arithmetic, attend_back(): weights = jnp.exp(scores - row_max)  21.7 us
    convert_element_type x1, other arithmetic, attend_back(): (scaling * probs * (prob_grad - row_delta)).astype(jnp.bfloat16)  18.8 us
    unnamed x26, local copies, waits for them, and re-layouts  15.2 us
    dot_general x1, matrix products, attend_back(): jnp.einsum('qhd,khd->hqk', grad_heads, values_all, preferred_element_type...  14.3 us
    dot_general x1, matrix products, attend_back(): jnp.einsum('qhd,khd->hqk', query_heads, keys_all, preferred_element_type=...  13.4 us
    dot_general x1, matrix products, attend_back(): jnp.einsum('hqk,qhd->khd', probs_low, grad_heads, preferred_element_type=...  10.3 us
    dot_general x1, matrix products, attend_back(): jnp.einsum('hqk,khd->qhd', probs_low, values_all, preferred_element_type=...  9.36 us
  transfers between devices with their start and end apart: 1, of which 1 were waited for; matrix products, arithmetic and copies ran while one was open for 24% of the time, Pallas kernels for 0%

commit v1 on v0

v1 whole, which is shorter than its diff:
```python
import functools

import jax
import jax.numpy as jnp
from jax import lax
from jax.experimental import pallas as pl
from jax.experimental.pallas import tpu as pltpu
from jax.sharding import PartitionSpec as P

HEADS = 16
GROUP = 8
BLOCK = 16
LOG2E = 1.4426950408889634


def dot(a, b, contract):
    return lax.dot_general(a, b, (contract, ((), ())), preferred_element_type=jnp.float32)


def hidden(pad, prefix_visible, keys, first_query, queries):
    rows = lax.broadcasted_iota(jnp.int32, (keys, queries), 0)
    cols = lax.broadcasted_iota(jnp.int32, (keys, queries), 1) + first_query
    return jnp.where(rows < pad, rows + 1 - prefix_visible, rows - pad - cols) > 0


def spans(tokens):
    size = tokens // 2 if tokens % 256 == 0 else tokens
    return [(start, size) for start in range(0, tokens, size)]


def fwd_kernel(sums, head_size, q_ref, k_ref, v_ref, pk_ref, pv_ref, attn_ref, max_ref, inv_ref):
    tokens, pad = q_ref.shape[0], pk_ref.shape[0]
    visible = lax.axis_index("seg") * sums
    scale = head_size**-0.5 * LOG2E
    for start, size in spans(tokens):
        own = start + size
        mask = hidden(pad, visible, pad + own, start, size)
        for head in range(q_ref.shape[1] // head_size):
            lanes = slice(head * head_size, (head + 1) * head_size)
            keys = jnp.concatenate([pk_ref[:, lanes], k_ref[:own, lanes]], 0)
            values = jnp.concatenate([pv_ref[:, lanes], v_ref[:own, lanes]], 0)
            scores = dot(keys, q_ref[start:own, lanes], ((1,), (1,)))
            scores = jnp.where(mask, jnp.float32(-1e30), scores)
            top = jnp.max(scores, 0, keepdims=True)
            weights = jnp.exp2((scores - top) * scale)
            inverse = 1.0 / jnp.sum(weights, 0, keepdims=True)
            probs_low = (weights * inverse).astype(jnp.bfloat16)
            attn = dot(values, probs_low, ((0,), (0,)))
            attn_ref[lanes, start:own] = attn.astype(jnp.bfloat16)
            max_ref[head : head + 1, start:own] = top
            inv_ref[head : head + 1, start:own] = inverse


def bwd_kernel(
    sums,
    head_size,
    q_ref,
    k_ref,
    v_ref,
    pk_ref,
    pv_ref,
    g_ref,
    max_ref,
    inv_ref,
    dq_ref,
    dk_ref,
    dv_ref,
    dpk_ref,
    dpv_ref,
    dq_t,
):
    tokens, pad = q_ref.shape[0], pk_ref.shape[0]
    visible = lax.axis_index("seg") * sums
    scaling = head_size**-0.5
    parts = spans(tokens)
    masks = [hidden(pad, visible, pad + start + size, start, size) for start, size in parts]
    for head in range(q_ref.shape[1] // head_size):
        lanes = slice(head * head_size, (head + 1) * head_size)
        key_sum, value_sum = [], []
        for (start, size), mask in zip(parts, masks):
            own = start + size
            keys = jnp.concatenate([pk_ref[:, lanes], k_ref[:own, lanes]], 0)
            values = jnp.concatenate([pv_ref[:, lanes], v_ref[:own, lanes]], 0)
            query, grad = q_ref[start:own, lanes], g_ref[start:own, lanes]
            scores = dot(keys, query, ((1,), (1,)))
            scores = jnp.where(mask, jnp.float32(-1e30), scores)
            top = max_ref[head : head + 1, start:own]
            inverse = inv_ref[head : head + 1, start:own]
            probs = jnp.exp2((scores - top) * (scaling * LOG2E)) * inverse
            prob_grad = dot(values, grad, ((1,), (1,)))
            weighted = probs * prob_grad
            row_delta = jnp.sum(weighted, 0, keepdims=True)
            score_grad = (scaling * (weighted - probs * row_delta)).astype(jnp.bfloat16)
            probs_low = probs.astype(jnp.bfloat16)
            dq_t[lanes, start:own] = dot(keys, score_grad, ((0,), (0,)))
            key_sum.append(dot(score_grad, query, ((1,), (0,))))
            value_sum.append(dot(probs_low, grad, ((1,), (0,))))
        for sum_list, own_ref, prompt_ref in (
            (key_sum, dk_ref, dpk_ref),
            (value_sum, dv_ref, dpv_ref),
        ):
            total = sum_list[-1]
            for part in sum_list[:-1]:
                count = part.shape[0]
                total = jnp.concatenate([total[:count] + part, total[count:]], 0)
            prompt_ref[:, lanes] = total[:pad].astype(jnp.bfloat16)
            own_ref[:, lanes] = total[pad:].astype(jnp.bfloat16)
    dq_ref[...] = dq_t[...].T.astype(jnp.bfloat16)


def lanes_block(rows, width):
    return pl.BlockSpec((rows, width), lambda g: (0, g))


def rows_block(rows, width):
    return pl.BlockSpec((rows, width), lambda g: (g, 0))


def shards(n_seg, n_dp, query, key, value, prompt_keys, prompt_values, out_grad, w_out):
    query, key, value, out_grad = query[0], key[0], value[0], out_grad[0]
    tokens, width = query.shape
    sums = prompt_keys.shape[1]
    head_size = width // HEADS
    group = GROUP * head_size
    read = (n_seg - 1) * sums
    pad = -(-read // 64) * 64
    prompts = jnp.stack([prompt_keys[0], prompt_values[0]])
    prompts = lax.all_gather(prompts, "seg", axis=1, tiled=True)[:, :read]
    prompts = jnp.pad(prompts, ((0, 0), (0, pad - read), (0, 0)))
    prompt_k, prompt_v = prompts[0], prompts[1]
    params = pltpu.CompilerParams(vmem_limit_bytes=48 * 1024 * 1024)
    own_spec, prompt_spec = lanes_block(tokens, group), lanes_block(pad, group)
    stat_spec = rows_block(GROUP, tokens)
    stat = jax.ShapeDtypeStruct((HEADS, tokens), jnp.float32)
    low = functools.partial(jax.ShapeDtypeStruct, dtype=jnp.bfloat16)
    flops = 2 * HEADS * tokens * tokens * head_size

    attn_t, top, inverse = pl.pallas_call(
        functools.partial(fwd_kernel, sums, head_size),
        grid=(HEADS // GROUP,),
        in_specs=[own_spec] * 3 + [prompt_spec] * 2,
        out_specs=[rows_block(group, tokens), stat_spec, stat_spec],
        out_shape=[low((width, tokens)), stat, stat],
        compiler_params=params,
        cost_estimate=pl.CostEstimate(
            flops=10 * flops, bytes_accessed=8 * tokens * width, transcendentals=0
        ),
    )(query, key, value, prompt_k, prompt_v)

    plan = split_plan(n_seg, n_dp, width, out_grad.shape[1])
    if plan is None:
        weight_grad = plain_weight(attn_t, out_grad)
    else:
        weight_grad = sum_weight(n_seg, n_dp, plan, attn_t, out_grad)

    head_low = jnp.einsum("td,hd->th", out_grad, w_out, preferred_element_type=jnp.float32)
    query_grad, key_grad, value_grad, pk_part, pv_part = pl.pallas_call(
        functools.partial(bwd_kernel, sums, head_size),
        grid=(HEADS // GROUP,),
        in_specs=[own_spec] * 3 + [prompt_spec] * 2 + [own_spec, stat_spec, stat_spec],
        out_specs=[own_spec] * 3 + [prompt_spec] * 2,
        out_shape=[low((tokens, width))] * 3 + [low((pad, width))] * 2,
        scratch_shapes=[pltpu.VMEM((group, tokens), jnp.float32)],
        compiler_params=params,
        cost_estimate=pl.CostEstimate(
            flops=25 * flops, bytes_accessed=16 * tokens * width, transcendentals=0
        ),
    )(query, key, value, prompt_k, prompt_v, head_low.astype(jnp.bfloat16), top, inverse)

    parts = jnp.stack([pk_part, pv_part])
    segment = lax.axis_index("seg")
    later = jnp.zeros((2, sums, width), jnp.float32)
    for step in range(1, n_seg):
        start = jnp.maximum(segment - step, 0) * sums
        block = lax.dynamic_slice_in_dim(parts, start, sums, 1)
        pairs = [(at, at - step) for at in range(step, n_seg)]
        later = later + lax.ppermute(block, "seg", pairs).astype(jnp.float32)
    later = later.astype(jnp.bfloat16)

    return (
        query_grad[None],
        key_grad[None],
        value_grad[None],
        later[0][None],
        later[1][None],
        weight_grad,
    )


def plain_weight(attn_t, out_grad):
    part = jnp.dot(attn_t, out_grad, preferred_element_type=jnp.float32)
    total = lax.psum(part, ("seg", "dp"))
    rms = jnp.sqrt(jnp.mean(total * total) + 1e-06)
    return (total * jnp.minimum(1.0, 1.0 / rms)).astype(jnp.bfloat16)


def split_plan(n_seg, n_dp, rows, cols):
    bits = n_dp.bit_length() - 1
    if n_seg != 2 or n_dp != 1 << bits or bits < 2 or rows % 64:
        return None
    rows, dims = rows // 4, []
    for _ in range(bits):
        if cols % 256 == 0:
            cols, dims = cols // 2, dims + [1]
        elif rows % 32 == 0:
            rows, dims = rows // 2, dims + [0]
        else:
            return None
    order = list(range(bits))
    return [list(zip(order, dims)), list(zip([1, 0] + order[2:], dims))]


def region(ref, at, shape):
    return ref.at[
        pl.ds(pl.multiple_of(at[0], 16), shape[0]), pl.ds(pl.multiple_of(at[1], 128), shape[1])
    ]


def stage_shapes(shape, plan):
    shapes = []
    for _, dim in plan:
        shape = (shape[0] // 2, shape[1]) if dim == 0 else (shape[0], shape[1] // 2)
        shapes.append(shape)
    return shapes


def by_rows(rows, body):
    block = next(size for size in (80, 64, 48, 32, 16) if rows % size == 0)

    @pl.loop(0, rows // block)
    def _(i):
        body(pl.multiple_of(i * block, BLOCK), block)


def sum_kernel(plans, attn_ref, grad_ref, out_ref, acc, core_out, core_in, gath, square_out, square_in, *rest):
    n_bits = len(plans[0])
    parts = len(plans)
    sends = [rest[p * n_bits : (p + 1) * n_bits] for p in range(parts)]
    recvs = [rest[(parts + p) * n_bits : (parts + p + 1) * n_bits] for p in range(parts)]
    send_sem, recv_sem = rest[2 * parts * n_bits :]
    seg, dp = lax.axis_index("seg"), lax.axis_index("dp")
    half, cols = acc.shape
    bit = [dp // (1 << b) % 2 for b in range(n_bits)]
    partner = [(seg, dp + (1 << b) * (1 - 2 * bit[b])) for b in range(n_bits)]
    other = (1 - seg, dp)
    count = [0]

    def send(source, target, device):
        at = count[0]
        count[0] += 1
        copy = pltpu.make_async_remote_copy(
            src_ref=source,
            dst_ref=target,
            send_sem=send_sem.at[at],
            recv_sem=recv_sem.at[at],
            device_id=device,
            device_id_type=pl.DeviceIdType.MESH,
        )
        copy.start()
        return copy

    barrier = pltpu.get_barrier_semaphore()
    for device in [other] + partner:
        pl.semaphore_signal(barrier, inc=1, device_id=device, device_id_type=pl.DeviceIdType.MESH)
    pl.semaphore_wait(barrier, 1 + n_bits)

    pieces = 4
    piece = half // pieces
    core = []
    for i in range(pieces):
        rows = pl.ds(pl.multiple_of((1 - seg) * half + i * piece, BLOCK), piece)
        core_out[i] = dot(attn_ref[rows, :], grad_ref[...], ((1,), (0,))).astype(jnp.bfloat16)
        core.append(send(core_out.at[i], core_in.at[i], other))
    for i in range(pieces):
        rows = pl.ds(pl.multiple_of(seg * half + i * piece, BLOCK), piece)
        acc[i * piece : (i + 1) * piece, :] = dot(attn_ref[rows, :], grad_ref[...], ((1,), (0,)))
    for i in range(pieces):
        core[i].wait()

        def add(row, block):
            acc[pl.ds(i * piece + row, block), :] += core_in[i, pl.ds(row, block), :].astype(
                jnp.float32
            )

        by_rows(piece, add)

    places = [(p * (half // parts), 0) for p in range(parts)]
    history = [[] for _ in range(parts)]
    for stage in range(n_bits):
        copies = []
        for p in range(parts):
            b, dim = plans[p][stage]
            shape = sends[p][stage].shape
            at = places[p]
            step = shape[dim]
            keep, give = [
                tuple(at[d] + (which * step if d == dim else 0) for d in range(2))
                for which in (bit[b], 1 - bit[b])
            ]
            lanes = pl.ds(pl.multiple_of(give[1], 128), shape[1])

            def cast(row, block):
                rows = pl.ds(pl.multiple_of(give[0] + row, BLOCK), block)
                sends[p][stage][pl.ds(row, block), :] = acc[rows, lanes].astype(jnp.bfloat16)

            by_rows(shape[0], cast)
            copies.append(send(sends[p][stage], recvs[p][stage], partner[b]))
            history[p].append((b, keep, shape))
            places[p] = keep
        for p in range(parts):
            copies[p].wait()
            _, keep, shape = history[p][stage]
            lanes = pl.ds(pl.multiple_of(keep[1], 128), shape[1])

            def add(row, block):
                rows = pl.ds(pl.multiple_of(keep[0] + row, BLOCK), block)
                acc[rows, lanes] += recvs[p][stage][pl.ds(row, block), :].astype(jnp.float32)

            by_rows(shape[0], add)

    squares = jnp.zeros((1, 1), jnp.float32)
    for p in range(parts):
        _, keep, shape = history[p][-1]
        own = region(acc, keep, shape)[...]
        squares = squares + jnp.sum(own * own, keepdims=True)
        region(gath, (seg * half + keep[0], keep[1]), shape)[...] = own.astype(jnp.bfloat16)
    square_out[0] = jnp.broadcast_to(squares, square_out.shape[1:])

    for stage in reversed(range(n_bits)):
        step = n_bits - 1 - stage
        copies = [send(square_out.at[step], square_in.at[step], partner[plans[0][stage][0]])]
        for p in range(parts):
            b, keep, shape = history[p][stage]
            mine = region(gath, (seg * half + keep[0], keep[1]), shape)
            copies.append(send(mine, mine, partner[b]))
        for copy in copies:
            copy.wait()
        square_out[step + 1] = square_out[step] + square_in[step]
    step = n_bits
    copies = [send(square_out.at[step], square_in.at[step], other)]
    mine = gath.at[pl.ds(pl.multiple_of(seg * half, BLOCK), half), :]
    copies.append(send(mine, mine, other))
    for copy in copies:
        copy.wait()
    total = square_out[step] + square_in[step]
    rms = jnp.sqrt(total[:1, :1] / (2 * half * cols) + 1e-06)
    factor = jnp.minimum(1.0, 1.0 / rms)

    def finish(row, block):
        rows = pl.ds(row, block)
        out_ref[rows, :] = (gath[rows, :].astype(jnp.float32) * factor).astype(jnp.bfloat16)

    by_rows(2 * half, finish)


def sum_weight(n_seg, n_dp, plans, attn_t, out_grad):
    width, cols = attn_t.shape[0], out_grad.shape[1]
    half, bits = width // 2, len(plans[0])
    low = functools.partial(pltpu.VMEM, dtype=jnp.bfloat16)
    shapes = [stage_shapes((half // len(plans), cols), plan) for plan in plans]
    buffers = [low(shape) for part in shapes for shape in part]
    copies = 4 + len(plans) * bits + (len(plans) + 1) * bits + 2
    vmem = pl.BlockSpec(memory_space=pltpu.VMEM)
    return pl.pallas_call(
        functools.partial(sum_kernel, plans),
        in_specs=[vmem] * 2,
        out_specs=vmem,
        out_shape=jax.ShapeDtypeStruct((width, cols), jnp.bfloat16),
        scratch_shapes=[
            pltpu.VMEM((half, cols), jnp.float32),
            low((4, half // 4, cols)),
            low((4, half // 4, cols)),
            low((width, cols)),
            pltpu.VMEM((bits + 1, 8, 128), jnp.float32),
            pltpu.VMEM((bits + 1, 8, 128), jnp.float32),
            *buffers,
            *buffers,
            pltpu.SemaphoreType.DMA((copies,)),
            pltpu.SemaphoreType.DMA((copies,)),
        ],
        compiler_params=pltpu.CompilerParams(
            collective_id=0, has_side_effects=True, vmem_limit_bytes=56 * 1024 * 1024
        ),
        cost_estimate=pl.CostEstimate(
            flops=2 * width * cols * attn_t.shape[1],
            bytes_accessed=4 * width * cols,
            transcendentals=0,
        ),
    )(attn_t, out_grad)


def solution(mesh):
    row = P("dp", "seg", None)
    return jax.shard_map(
        functools.partial(shards, mesh.shape["seg"], mesh.shape["dp"]),
        mesh=mesh,
        in_specs=(row,) * 6 + (P(),),
        out_specs=(row,) * 5 + (P(),),
        check_vma=False,
    )
```

time: 339 us -> 175 us (0.52)
  Pallas kernels: 0 us -> 154 us
  waiting for transfers between devices: 152 us -> 0.01 us
  matrix products: 76.4 us -> 6.58 us
  other arithmetic: 60.3 us -> 0.76 us
  local copies, waits for them, and re-layouts: 25.6 us -> 9.45 us
  between operations: 14.9 us -> 0.79 us
  blocking collectives: 8.77 us -> 2.25 us
    pallas_call x0 -> x3, Pallas kernels: none -> 154 us  [the longest x1 120 us: sum_weight(): pl.pallas_call(functools.partial(sum_kernel, plans), in_specs=[vmem] * 2,...]
    psum x1 -> x0, waiting for transfers between devices: 152 us -> none  [shards(): weight_total = lax.psum(weight_part, ('seg', 'dp'))]
    dot_general x8 -> x1, matrix products: 76.4 us -> 6.58 us  [shards(): jnp.einsum('td,hd->th', out_grad, w_out, preferred_element_type=jnp.float32)]
    convert_element_type x2 -> x0, other arithmetic: 28.1 us -> none  [the longest x1 18.8 us: attend_back(): (scaling * probs * (prob_grad - row_delta)).astype(jnp.bfloat16)]
    sub x2 -> x0, other arithmetic: 21.7 us -> none  [the longest x1 21.7 us: attend_back(): weights = jnp.exp(scores - row_max)]
    reduce_sum x1 -> x0, other arithmetic: 8.7 us -> none  [shards(): rms_value = jnp.sqrt(jnp.mean(weight_total * weight_total) + 1e-06)]
    unnamed x26 -> x15, local copies, waits for them, and re-layouts: 15.2 us -> 8.47 us
    all_gather x4 -> x1, blocking collectives: 8.77 us -> 2.25 us  [shards(): prompts = lax.all_gather(prompts, 'seg', axis=1, tiled=True)[:, :read]]
  transfers between devices with their start and end apart: 1 -> 1, of which waited for: 1 -> 0; matrix products, arithmetic and copies ran while one was open for 24% -> 0% of each run, Pallas kernels for 0% -> 69%
where the time goes in v1:
time: 175 us
  Pallas kernels  154 us (88%)
  local copies, waits for them, and re-layouts  9.45 us (5%)
  matrix products  6.58 us (4%)
  blocking collectives  2.25 us (1%)
    pallas_call x1, Pallas kernels, sum_weight(): pl.pallas_call(functools.partial(sum_kernel, plans), in_specs=[vmem] * 2,...  120 us
    pallas_call x1, Pallas kernels, shards(): pl.pallas_call(functools.partial(bwd_kernel, sums, head_size), grid=(HEAD...  18.8 us
    pallas_call x1, Pallas kernels, shards(): pl.pallas_call(functools.partial(fwd_kernel, sums, head_size), grid=(HEAD...  14.8 us
    unnamed x15, local copies, waits for them, and re-layouts  8.47 us
    dot_general x1, matrix products, shards(): jnp.einsum('td,hd->th', out_grad, w_out, preferred_element_type=jnp.float32)  6.58 us
  transfers between devices with their start and end apart: 1, of which 0 were waited for; matrix products, arithmetic and copies ran while one was open for 0% of the time, Pallas kernels for 69%

profile of v1, /device:TPU:0, one launch (start us, length us, event | category | flops | bytes accessed | tf_op | source)
XLA Modules:
  0.0 174.6 jit_solution(11677083591601998140)
XLA Ops:
  0.6 0.0 copy-start.4
  0.6 0.0 copy-start.5
  0.7 1.3 copy.13
  1.9 1.1 copy.14
  3.0 0.6 pad_maximum_fusion
  3.6 2.3 %all_gather.3 = bf16[2,100,1280]{2,0,1:T(2,128)(2,1)S(1)} all-gather(bf16[2,50,1280]{2,0,1:T(2,128)(2,1)S(1)} %pad_maximum_fusion), channel_id=1, replica_groups=mesh['seg'=2,'dp'=16] {'seg'}, dimensions={1}, use_global_device_ids=true | all-gather | bytes 768000 | tf_op jit(solution)/shard_map/all_gather | solution.py:128
  5.9 0.2 slice.21
  6.1 0.0 copy-done.4
  6.1 0.1 copy_select_fusion
  6.2 0.0 copy-done.5
  6.3 0.0 copy-start
  6.3 0.0 copy-start.1
  6.3 0.0 copy-start.2
  6.3 6.6 %convolution_convert_fusion.g_ref = bf16[512,1280]{1,0:T(8,128)(2,1)S(1)} fusion(bf16[1280,2560]{1,0:T(8,128)(2,1)} %param.13, bf16[1,512,2560]{2,1,0:T(8,128)(2,1)S(1)} %copy-done.5), kind=kOutput, calls=%fused_computation | convolution fusion | flops 3356098560 | bytes 10485760 | tf_op jit(solution)/shard_map/td,hd->th/dot_general | solution.py:156
  12.9 0.0 copy-done
  12.9 0.0 copy-done.1
  12.9 0.0 copy-done.2
  12.9 14.8 %shard_map.118 = (bf16[1280,512]{1,0:T(8,128)(2,1)S(1)}, f32[16,512]{1,0:T(8,128)S(1)}, f32[16,512]{1,0:T(8,128)S(1)}) custom-call(bf16[512,1280]{1,0:T(8,128)(2,1)S(1)} %bitcast.18, bf16[512,1280]{1,0:T(8,128)(2,1)S(1)} %bitcast.20, bf16[512,1280]{1,0:T(8,128)(2,1)S(1)} %bitcast.22, bf16[64,1280]{1,0:T(8,128)(2,1)S(1)} %get-tuple-element.23.pk_ref, ...), custom_call_target="tpu_custom_call" | custom-call | flops 6710886400 | bytes 5242880 | tf_op jit(solution)/shard_map/pallas_call | solution.py:138
  27.7 0.0 copy-start.3
  27.7 18.8 %shard_map.119 = (bf16[512,1280]{1,0:T(8,128)(2,1)}, bf16[512,1280]{1,0:T(8,128)(2,1)}, bf16[512,1280]{1,0:T(8,128)(2,1)}, bf16[64,1280]{1,0:T(8,128)(2,1)S(1)}, bf16[64,1280]{1,0:T(8,128)(2,1)S(1)}) custom-call(bf16[512,1280]{1,0:T(8,128)(2,1)S(1)} %bitcast.19, bf16[512,1280]{1,0:T(8,128)(2,1)S(1)} %bitcast.21, bf16[512,1280]{1,0:T(8,128)(2,1)S(1)} %bitcast.23, ...), custom_call_target="tpu_custom_call" | custom-call | flops 16777216000 | bytes 10485760 | tf_op jit(solution)/shard_map/pallas_call | solution.py:157
  46.5 0.0 copy-done.3
  46.5 0.1 fusion
  46.6 1.3 collective-permute-start
  47.9 119.9 %shard_map.120 = bf16[1280,2560]{1,0:T(8,128)(2,1)} custom-call(bf16[1280,512]{1,0:T(8,128)(2,1)} %copy-done.3, bf16[512,2560]{1,0:T(8,128)(2,1)} %bitcast.24), custom_call_target="tpu_custom_call" | custom-call | flops 3355443200 | bytes 13107200 | tf_op jit(solution)/shard_map/pallas_call | solution.py:364
  167.8 0.0 collective-permute-done
  167.8 0.7 fusion.2
  168.6 6.1 %copy.19 = bf16[1280,2560]{1,0:T(8,128)(2,1)} copy(bf16[1280,2560]{1,0:T(8,128)(2,1)} %shard_map.120) | data formatting | bytes 13107200
  (1 shorter events, 0.0 us)
Async XLA Ops:
  0.6 5.5 %copy-start.4 = (pred[64]{0:T(512)(128)(4,1)S(1)}, pred[64]{0:T(512)(128)(4,1)}, u32[]{:S(2)}) copy-start(pred[64]{0:T(512)(128)(4,1)} %constant.5.clone.1) | copy-start | bytes 196
  0.6 5.6 %copy-start.5 = (bf16[1,512,2560]{2,1,0:T(8,128)(2,1)S(1)}, bf16[1,512,2560]{2,1,0:T(8,128)(2,1)}, u32[]{:S(2)}) copy-start(bf16[1,512,2560]{2,1,0:T(8,128)(2,1)} %param.12) | copy-start | bytes 7864324
  6.3 6.6 %copy-start = (bf16[1,512,1280]{2,1,0:T(8,128)(2,1)S(1)}, bf16[1,512,1280]{2,1,0:T(8,128)(2,1)}, u32[]{:S(2)}) copy-start(bf16[1,512,1280]{2,1,0:T(8,128)(2,1)} %param.7) | copy-start | bytes 3932164
  6.3 6.6 %copy-start.1 = (bf16[1,512,1280]{2,1,0:T(8,128)(2,1)S(1)}, bf16[1,512,1280]{2,1,0:T(8,128)(2,1)}, u32[]{:S(2)}) copy-start(bf16[1,512,1280]{2,1,0:T(8,128)(2,1)} %param.8) | copy-start | bytes 3932164
  6.3 6.6 %copy-start.2 = (bf16[1,512,1280]{2,1,0:T(8,128)(2,1)S(1)}, bf16[1,512,1280]{2,1,0:T(8,128)(2,1)}, u32[]{:S(2)}) copy-start(bf16[1,512,1280]{2,1,0:T(8,128)(2,1)} %param.9) | copy-start | bytes 3932164
  27.7 18.9 %copy-start.3 = (bf16[1280,512]{1,0:T(8,128)(2,1)}, bf16[1280,512]{1,0:T(8,128)(2,1)S(1)}, u32[]{:S(2)}) copy-start(bf16[1280,512]{1,0:T(8,128)(2,1)S(1)} %get-tuple-element.21.attn_ref) | copy-start | bytes 3932164
  46.6 121.2 %collective-permute-start = (bf16[2,50,1280]{2,1,0:T(8,128)(2,1)S(1)}, bf16[2,50,1280]{2,1,0:T(8,128)(2,1)S(1)}, u32[]{:S(2)}, u32[]{:S(2)}) collective-permute-start(bf16[2,50,1280]{2,1,0:T(8,128)(2,1)S(1)} %fusion), channel_id=1, source_target_pairs={{16,0},{17,1},{18,2},{19,3},{20,4},{21,5},{22,6},{23,7},{24,8},{25... | collective-permute-start | bytes 768008 | tf_op jit(solution)/shard_map/ppermute | solution.py:177

commit v2 on v1

--- a/solution.py
+++ b/solution.py
@@ -196,18 +196,22 @@
 
 def split_plan(n_seg, n_dp, rows, cols):
     bits = n_dp.bit_length() - 1
-    if n_seg != 2 or n_dp != 1 << bits or bits < 2 or rows % 64:
+    if n_seg != 2 or n_dp != 1 << bits or bits < 3:
         return None
-    rows, dims = rows // 4, []
-    for _ in range(bits):
-        if cols % 256 == 0:
-            cols, dims = cols // 2, dims + [1]
-        elif rows % 32 == 0:
-            rows, dims = rows // 2, dims + [0]
-        else:
-            return None
     order = list(range(bits))
-    return [list(zip(order, dims)), list(zip([1, 0] + order[2:], dims))]
+    orders = [order, [1, 0] + order[2:], [2, 0, 1] + order[3:]]
+    for parts in (5, 4, 3, 2, 1):
+        size, width, dims = rows // (2 * parts), cols, []
+        if rows % (2 * parts * BLOCK):
+            continue
+        for _ in range(bits):
+            if width % 256 == 0:
+                width, dims = width // 2, dims + [1]
+            elif size % (2 * BLOCK) == 0:
+                size, dims = size // 2, dims + [0]
+        if len(dims) == bits:
+            return [list(zip(orders[part % 3], dims)) for part in range(parts)]
+    return None
 
 
 def region(ref, at, shape):
@@ -225,25 +229,26 @@
 
 
 def by_rows(rows, body):
-    block = next(size for size in (80, 64, 48, 32, 16) if rows % size == 0)
+    block = next(size for size in (64, 48, 32, 16) if rows % size == 0)
 
     @pl.loop(0, rows // block)
     def _(i):
         body(pl.multiple_of(i * block, BLOCK), block)
 
 
-def sum_kernel(plans, attn_ref, grad_ref, out_ref, acc, core_out, core_in, gath, square_out, square_in, *rest):
+def sum_kernel(plans, attn_ref, grad_ref, out_ref, square_ref, acc, core_out, core_in, gath, square_out, square_in, *rest):
     n_bits = len(plans[0])
     parts = len(plans)
     sends = [rest[p * n_bits : (p + 1) * n_bits] for p in range(parts)]
     recvs = [rest[(parts + p) * n_bits : (parts + p + 1) * n_bits] for p in range(parts)]
-    send_sem, recv_sem = rest[2 * parts * n_bits :]
+    send_sem, recv_sem, local_sem = rest[2 * parts * n_bits :]
     seg, dp = lax.axis_index("seg"), lax.axis_index("dp")
-    half, cols = acc.shape
+    half = acc.shape[0]
+    size = half // parts
     bit = [dp // (1 << b) % 2 for b in range(n_bits)]
     partner = [(seg, dp + (1 << b) * (1 - 2 * bit[b])) for b in range(n_bits)]
     other = (1 - seg, dp)
-    count = [0]
+    count = [0, 0]
 
     def send(source, target, device):
         at = count[0]
@@ -259,117 +264,132 @@
         copy.start()
         return copy
 
+    def part_rows(side, p):
+        return pl.ds(pl.multiple_of(side * half + p * size, BLOCK), size)
+
+    def store(side, p):
+        at = count[1]
+        count[1] += 1
+        rows = part_rows(side, p)
+        copy = pltpu.make_async_copy(gath.at[rows, :], out_ref.at[rows, :], local_sem.at[at])
+        copy.start()
+        return copy
+
     barrier = pltpu.get_barrier_semaphore()
     for device in [other] + partner:
         pl.semaphore_signal(barrier, inc=1, device_id=device, device_id_type=pl.DeviceIdType.MESH)
     pl.semaphore_wait(barrier, 1 + n_bits)
 
-    pieces = 4
-    piece = half // pieces
     core = []
-    for i in range(pieces):
-        rows = pl.ds(pl.multiple_of((1 - seg) * half + i * piece, BLOCK), piece)
-        core_out[i] = dot(attn_ref[rows, :], grad_ref[...], ((1,), (0,))).astype(jnp.bfloat16)
-        core.append(send(core_out.at[i], core_in.at[i], other))
-    for i in range(pieces):
-        rows = pl.ds(pl.multiple_of(seg * half + i * piece, BLOCK), piece)
-        acc[i * piece : (i + 1) * piece, :] = dot(attn_ref[rows, :], grad_ref[...], ((1,), (0,)))
-    for i in range(pieces):
-        core[i].wait()
-
-        def add(row, block):
-            acc[pl.ds(i * piece + row, block), :] += core_in[i, pl.ds(row, block), :].astype(
-                jnp.float32
-            )
-
-        by_rows(piece, add)
-
-    places = [(p * (half // parts), 0) for p in range(parts)]
+    for p in range(parts):
+        product = dot(attn_ref[part_rows(1 - seg, p), :], grad_ref[...], ((1,), (0,)))
+        core_out[p] = product.astype(jnp.bfloat16)
+        core.append(send(core_out.at[p], core_in.at[p], other))
+    places = [(p * size, 0) for p in range(parts)]
     history = [[] for _ in range(parts)]
+    flying = [None] * parts
     for stage in range(n_bits):
-        copies = []
         for p in range(parts):
+            if stage == 0:
+                acc[p * size : (p + 1) * size, :] = dot(
+                    attn_ref[part_rows(seg, p), :], grad_ref[...], ((1,), (0,))
+                )
+                core[p].wait()
+                arrived, at, shape = core_in.at[p], places[p], (size, acc.shape[1])
+            else:
+                flying[p].wait()
+                arrived, (_, at, shape) = recvs[p][stage - 1], history[p][-1]
+            add_arrived(acc, arrived, at, shape)
             b, dim = plans[p][stage]
             shape = sends[p][stage].shape
-            at = places[p]
-            step = shape[dim]
             keep, give = [
-                tuple(at[d] + (which * step if d == dim else 0) for d in range(2))
+                tuple(at[d] + (which * shape[d] if d == dim else 0) for d in range(2))
                 for which in (bit[b], 1 - bit[b])
             ]
-            lanes = pl.ds(pl.multiple_of(give[1], 128), shape[1])
-
-            def cast(row, block):
-                rows = pl.ds(pl.multiple_of(give[0] + row, BLOCK), block)
-                sends[p][stage][pl.ds(row, block), :] = acc[rows, lanes].astype(jnp.bfloat16)
-
-            by_rows(shape[0], cast)
-            copies.append(send(sends[p][stage], recvs[p][stage], partner[b]))
+            cast_given(acc, sends[p][stage], give, shape)
+            flying[p] = send(sends[p][stage], recvs[p][stage], partner[b])
             history[p].append((b, keep, shape))
-            places[p] = keep
-        for p in range(parts):
-            copies[p].wait()
-            _, keep, shape = history[p][stage]
-            lanes = pl.ds(pl.multiple_of(keep[1], 128), shape[1])
-
-            def add(row, block):
-                rows = pl.ds(pl.multiple_of(keep[0] + row, BLOCK), block)
-                acc[rows, lanes] += recvs[p][stage][pl.ds(row, block), :].astype(jnp.float32)
-
-            by_rows(shape[0], add)
+
+    def gather(p, stage):
+        b, keep, shape = history[p][stage]
+        mine = region(gath, (seg * half + keep[0], keep[1]), shape)
+        return send(mine, mine, partner[b])
 
     squares = jnp.zeros((1, 1), jnp.float32)
     for p in range(parts):
+        flying[p].wait()
         _, keep, shape = history[p][-1]
-        own = region(acc, keep, shape)[...]
+        own = region(acc, keep, shape)[...] + recvs[p][-1][...].astype(jnp.float32)
         squares = squares + jnp.sum(own * own, keepdims=True)
         region(gath, (seg * half + keep[0], keep[1]), shape)[...] = own.astype(jnp.bfloat16)
+        flying[p] = gather(p, n_bits - 1)
     square_out[0] = jnp.broadcast_to(squares, square_out.shape[1:])
-
+    square_copy = send(square_out.at[0], square_in.at[0], partner[0])
+
+    stores = []
     for stage in reversed(range(n_bits)):
+        for p in range(parts):
+            flying[p].wait()
+            if stage > 0:
+                flying[p] = gather(p, stage - 1)
+            else:
+                mine = gath.at[part_rows(seg, p), :]
+                flying[p] = send(mine, mine, other)
+                stores.append(store(seg, p))
         step = n_bits - 1 - stage
-        copies = [send(square_out.at[step], square_in.at[step], partner[plans[0][stage][0]])]
-        for p in range(parts):
-            b, keep, shape = history[p][stage]
-            mine = region(gath, (seg * half + keep[0], keep[1]), shape)
-            copies.append(send(mine, mine, partner[b]))
-        for copy in copies:
-            copy.wait()
+        square_copy.wait()
         square_out[step + 1] = square_out[step] + square_in[step]
-    step = n_bits
-    copies = [send(square_out.at[step], square_in.at[step], other)]
-    mine = gath.at[pl.ds(pl.multiple_of(seg * half, BLOCK), half), :]
-    copies.append(send(mine, mine, other))
-    for copy in copies:
+        device = partner[step + 1] if step + 1 < n_bits else other
+        square_copy = send(square_out.at[step + 1], square_in.at[step + 1], device)
+    square_copy.wait()
+    square_ref[...] = square_out[n_bits] + square_in[n_bits]
+    for p in range(parts):
+        flying[p].wait()
+        stores.append(store(1 - seg, p))
+    for copy in stores:
         copy.wait()
-    total = square_out[step] + square_in[step]
-    rms = jnp.sqrt(total[:1, :1] / (2 * half * cols) + 1e-06)
-    factor = jnp.minimum(1.0, 1.0 / rms)
-
-    def finish(row, block):
-        rows = pl.ds(row, block)
-        out_ref[rows, :] = (gath[rows, :].astype(jnp.float32) * factor).astype(jnp.bfloat16)
-
-    by_rows(2 * half, finish)
+
+
+def add_arrived(acc, arrived, at, shape):
+    lanes = pl.ds(pl.multiple_of(at[1], 128), shape[1])
+
+    def add(row, block):
+        rows = pl.ds(pl.multiple_of(at[0] + row, BLOCK), block)
+        acc[rows, lanes] += arrived[pl.ds(row, block), :].astype(jnp.float32)
+
+    by_rows(shape[0], add)
+
+
+def cast_given(acc, target, at, shape):
+    lanes = pl.ds(pl.multiple_of(at[1], 128), shape[1])
+
+    def cast(row, block):
+        rows = pl.ds(pl.multiple_of(at[0] + row, BLOCK), block)
+        target[pl.ds(row, block), :] = acc[rows, lanes].astype(jnp.bfloat16)
+
+    by_rows(shape[0], cast)
 
 
 def sum_weight(n_seg, n_dp, plans, attn_t, out_grad):
     width, cols = attn_t.shape[0], out_grad.shape[1]
-    half, bits = width // 2, len(plans[0])
+    half, bits, parts = width // 2, len(plans[0]), len(plans)
     low = functools.partial(pltpu.VMEM, dtype=jnp.bfloat16)
-    shapes = [stage_shapes((half // len(plans), cols), plan) for plan in plans]
+    shapes = [stage_shapes((half // parts, cols), plan) for plan in plans]
     buffers = [low(shape) for part in shapes for shape in part]
-    copies = 4 + len(plans) * bits + (len(plans) + 1) * bits + 2
+    copies = 2 * parts + 2 * parts * bits + bits + 1
     vmem = pl.BlockSpec(memory_space=pltpu.VMEM)
-    return pl.pallas_call(
+    total, squares = pl.pallas_call(
         functools.partial(sum_kernel, plans),
         in_specs=[vmem] * 2,
-        out_specs=vmem,
-        out_shape=jax.ShapeDtypeStruct((width, cols), jnp.bfloat16),
+        out_specs=[pl.BlockSpec(memory_space=pl.ANY), vmem],
+        out_shape=[
+            jax.ShapeDtypeStruct((width, cols), jnp.bfloat16),
+            jax.ShapeDtypeStruct((8, 128), jnp.float32),
+        ],
         scratch_shapes=[
             pltpu.VMEM((half, cols), jnp.float32),
-            low((4, half // 4, cols)),
-            low((4, half // 4, cols)),
+            low((parts, half // parts, cols)),
+            low((parts, half // parts, cols)),
             low((width, cols)),
             pltpu.VMEM((bits + 1, 8, 128), jnp.float32),
             pltpu.VMEM((bits + 1, 8, 128), jnp.float32),
@@ -377,6 +397,7 @@
             *buffers,
             pltpu.SemaphoreType.DMA((copies,)),
             pltpu.SemaphoreType.DMA((copies,)),
+            pltpu.SemaphoreType.DMA((2 * parts,)),
         ],
         compiler_params=pltpu.CompilerParams(
             collective_id=0, has_side_effects=True, vmem_limit_bytes=56 * 1024 * 1024
@@ -387,6 +408,8 @@
             transcendentals=0,
         ),
     )(attn_t, out_grad)
+    rms = jnp.sqrt(squares[0, 0] / (width * cols) + 1e-06)
+    return (total.astype(jnp.float32) * jnp.minimum(1.0, 1.0 / rms)).astype(jnp.bfloat16)
 
 
 def solution(mesh):

time: 175 us -> 149 us (0.85)
  Pallas kernels: 154 us -> 125 us
  other arithmetic: 0.76 us -> 7.62 us
  local copies, waits for them, and re-layouts: 9.45 us -> 4.57 us
    pallas_call x1, Pallas kernels: 120 us -> 91.6 us  [sum_weight(): pl.pallas_call(functools.partial(sum_kernel, plans), in_specs=[vmem] * 2,...]
    convert_element_type x0 -> x1, other arithmetic: none -> 6.86 us  [sum_weight(): (total.astype(jnp.float32) * jnp.minimum(1.0, 1.0 / rms)).astype(jnp.bflo...]
    unnamed x15 -> x14, local copies, waits for them, and re-layouts: 8.47 us -> 2.4 us
  transfers between devices with their start and end apart: 1 -> 1, of which waited for: 0 -> 0; matrix products, arithmetic and copies ran while one was open for 0% -> 5% of each run, Pallas kernels for 69% -> 61%
where the time goes in v2:
time: 149 us
  Pallas kernels  125 us (84%)
  other arithmetic  7.62 us (5%)
  matrix products  6.58 us (4%)
  local copies, waits for them, and re-layouts  4.57 us (3%)
  blocking collectives  2.25 us (2%)
    pallas_call x1, Pallas kernels, sum_weight(): pl.pallas_call(functools.partial(sum_kernel, plans), in_specs=[vmem] * 2,...  91.6 us
    pallas_call x1, Pallas kernels, shards(): pl.pallas_call(functools.partial(bwd_kernel, sums, head_size), grid=(HEAD...  18.8 us
    pallas_call x1, Pallas kernels, shards(): pl.pallas_call(functools.partial(fwd_kernel, sums, head_size), grid=(HEAD...  14.8 us
    convert_element_type x1, other arithmetic, sum_weight(): (total.astype(jnp.float32) * jnp.minimum(1.0, 1.0 / rms)).astype(jnp.bflo...  6.86 us
    dot_general x1, matrix products, shards(): jnp.einsum('td,hd->th', out_grad, w_out, preferred_element_type=jnp.float32)  6.58 us
  transfers between devices with their start and end apart: 1, of which 0 were waited for; matrix products, arithmetic and copies ran while one was open for 5% of the time, Pallas kernels for 61%

profile of v2, /device:TPU:0, one launch (start us, length us, event | category | flops | bytes accessed | tf_op | source)
XLA Modules:
  0.0 149.0 jit_solution(8603764699676843528)
XLA Ops:
  0.6 0.0 copy-start.4
  0.6 0.0 copy-start.5
  0.7 1.3 copy.13
  1.9 1.1 copy.14
  3.0 0.6 pad_maximum_fusion
  3.6 2.3 %all_gather.3 = bf16[2,100,1280]{2,0,1:T(2,128)(2,1)S(1)} all-gather(bf16[2,50,1280]{2,0,1:T(2,128)(2,1)S(1)} %pad_maximum_fusion), channel_id=1, replica_groups=mesh['seg'=2,'dp'=16] {'seg'}, dimensions={1}, use_global_device_ids=true | all-gather | bytes 768000 | tf_op jit(solution)/shard_map/all_gather | solution.py:128
  5.9 0.2 slice.25
  6.1 0.0 copy-done.4
  6.1 0.1 copy_select_fusion
  6.2 0.0 copy-done.5
  6.3 0.0 copy-start
  6.3 0.0 copy-start.1
  6.3 0.0 copy-start.2
  6.3 6.6 %convolution_convert_fusion.g_ref = bf16[512,1280]{1,0:T(8,128)(2,1)S(1)} fusion(bf16[1280,2560]{1,0:T(8,128)(2,1)} %param.13, bf16[1,512,2560]{2,1,0:T(8,128)(2,1)S(1)} %copy-done.5), kind=kOutput, calls=%fused_computation.1 | convolution fusion | flops 3356098560 | bytes 10485760 | tf_op jit(solution)/shard_map/td,hd->th/dot_general | solution.py:156
  12.9 0.0 copy-done
  12.9 0.0 copy-done.1
  12.9 0.0 copy-done.2
  12.9 14.8 %shard_map.118 = (bf16[1280,512]{1,0:T(8,128)(2,1)S(1)}, f32[16,512]{1,0:T(8,128)S(1)}, f32[16,512]{1,0:T(8,128)S(1)}) custom-call(bf16[512,1280]{1,0:T(8,128)(2,1)S(1)} %bitcast.19, bf16[512,1280]{1,0:T(8,128)(2,1)S(1)} %bitcast.21, bf16[512,1280]{1,0:T(8,128)(2,1)S(1)} %bitcast.23, bf16[64,1280]{1,0:T(8,128)(2,1)S(1)} %get-tuple-element.27.pk_ref, ...), custom_call_target="tpu_custom_call" | custom-call | flops 6710886400 | bytes 5242880 | tf_op jit(solution)/shard_map/pallas_call | solution.py:138
  27.7 0.0 copy-start.3
  27.7 18.8 %shard_map.119 = (bf16[512,1280]{1,0:T(8,128)(2,1)}, bf16[512,1280]{1,0:T(8,128)(2,1)}, bf16[512,1280]{1,0:T(8,128)(2,1)}, bf16[64,1280]{1,0:T(8,128)(2,1)S(1)}, bf16[64,1280]{1,0:T(8,128)(2,1)S(1)}) custom-call(bf16[512,1280]{1,0:T(8,128)(2,1)S(1)} %bitcast.20, bf16[512,1280]{1,0:T(8,128)(2,1)S(1)} %bitcast.22, bf16[512,1280]{1,0:T(8,128)(2,1)S(1)} %bitcast.24, ...), custom_call_target="tpu_custom_call" | custom-call | flops 16777216000 | bytes 10485760 | tf_op jit(solution)/shard_map/pallas_call | solution.py:157
  46.5 0.0 copy-done.3
  46.5 0.1 fusion
  46.6 1.3 collective-permute-start
  47.9 91.6 %shard_map.120 = (bf16[1280,2560]{1,0:T(8,128)(2,1)}, f32[8,128]{1,0:T(8,128)}) custom-call(bf16[1280,512]{1,0:T(8,128)(2,1)} %copy-done.3, bf16[512,2560]{1,0:T(8,128)(2,1)} %bitcast.25), custom_call_target="tpu_custom_call" | custom-call | flops 3355443200 | bytes 13107200 | tf_op jit(solution)/shard_map/pallas_call | solution.py:381
  139.5 1.2 slice.24
  141.4 6.9 %multiply_convert_fusion = bf16[1280,2560]{1,0:T(8,128)(2,1)} fusion(bf16[1280,2560]{1,0:T(8,128)(2,1)} %get-tuple-element.24, f32[]{:T(128)} %bitcast.11), kind=kLoop, calls=%fused_computation | loop fusion | flops 9830400 | bytes 13107204 | tf_op jit(solution)/shard_map/convert_element_type | solution.py:412
  148.3 0.0 collective-permute-done
  148.3 0.7 fusion.2
  (1 shorter events, 0.0 us)
Async XLA Ops:
  0.6 5.5 %copy-start.4 = (pred[64]{0:T(512)(128)(4,1)S(1)}, pred[64]{0:T(512)(128)(4,1)}, u32[]{:S(2)}) copy-start(pred[64]{0:T(512)(128)(4,1)} %constant.18.clone.1) | copy-start | bytes 196
  0.6 5.6 %copy-start.5 = (bf16[1,512,2560]{2,1,0:T(8,128)(2,1)S(1)}, bf16[1,512,2560]{2,1,0:T(8,128)(2,1)}, u32[]{:S(2)}) copy-start(bf16[1,512,2560]{2,1,0:T(8,128)(2,1)} %param.12) | copy-start | bytes 7864324
  6.3 6.6 %copy-start = (bf16[1,512,1280]{2,1,0:T(8,128)(2,1)S(1)}, bf16[1,512,1280]{2,1,0:T(8,128)(2,1)}, u32[]{:S(2)}) copy-start(bf16[1,512,1280]{2,1,0:T(8,128)(2,1)} %param.7) | copy-start | bytes 3932164
  6.3 6.6 %copy-start.1 = (bf16[1,512,1280]{2,1,0:T(8,128)(2,1)S(1)}, bf16[1,512,1280]{2,1,0:T(8,128)(2,1)}, u32[]{:S(2)}) copy-start(bf16[1,512,1280]{2,1,0:T(8,128)(2,1)} %param.8) | copy-start | bytes 3932164
  6.3 6.6 %copy-start.2 = (bf16[1,512,1280]{2,1,0:T(8,128)(2,1)S(1)}, bf16[1,512,1280]{2,1,0:T(8,128)(2,1)}, u32[]{:S(2)}) copy-start(bf16[1,512,1280]{2,1,0:T(8,128)(2,1)} %param.9) | copy-start | bytes 3932164
  27.7 18.9 %copy-start.3 = (bf16[1280,512]{1,0:T(8,128)(2,1)}, bf16[1280,512]{1,0:T(8,128)(2,1)S(1)}, u32[]{:S(2)}) copy-start(bf16[1280,512]{1,0:T(8,128)(2,1)S(1)} %get-tuple-element.23.attn_ref) | copy-start | bytes 3932164
  46.6 101.7 %collective-permute-start = (bf16[2,50,1280]{2,1,0:T(8,128)(2,1)S(1)}, bf16[2,50,1280]{2,1,0:T(8,128)(2,1)S(1)}, u32[]{:S(2)}, u32[]{:S(2)}) collective-permute-start(bf16[2,50,1280]{2,1,0:T(8,128)(2,1)S(1)} %fusion), channel_id=1, source_target_pairs={{16,0},{17,1},{18,2},{19,3},{20,4},{21,5},{22,6},{23,7},{24,8},{25... | collective-permute-start | bytes 768008 | tf_op jit(solution)/shard_map/ppermute | solution.py:177

commit v3 on v2

--- a/solution.py
+++ b/solution.py
@@ -51,60 +51,50 @@
             inv_ref[head : head + 1, start:own] = inverse
 
 
-def bwd_kernel(
-    sums,
-    head_size,
-    q_ref,
-    k_ref,
-    v_ref,
-    pk_ref,
-    pv_ref,
-    g_ref,
-    max_ref,
-    inv_ref,
-    dq_ref,
-    dk_ref,
-    dv_ref,
-    dpk_ref,
-    dpv_ref,
-    dq_t,
-):
+def bwd_head(sums, head_size, head, refs):
+    q_ref, k_ref, v_ref, pk_ref, pv_ref, g_ref, max_ref, inv_ref = refs[:8]
+    dk_ref, dv_ref, dpk_ref, dpv_ref, dq_t = refs[8:]
     tokens, pad = q_ref.shape[0], pk_ref.shape[0]
     visible = lax.axis_index("seg") * sums
     scaling = head_size**-0.5
     parts = spans(tokens)
     masks = [hidden(pad, visible, pad + start + size, start, size) for start, size in parts]
-    for head in range(q_ref.shape[1] // head_size):
-        lanes = slice(head * head_size, (head + 1) * head_size)
-        key_sum, value_sum = [], []
-        for (start, size), mask in zip(parts, masks):
-            own = start + size
-            keys = jnp.concatenate([pk_ref[:, lanes], k_ref[:own, lanes]], 0)
-            values = jnp.concatenate([pv_ref[:, lanes], v_ref[:own, lanes]], 0)
-            query, grad = q_ref[start:own, lanes], g_ref[start:own, lanes]
-            scores = dot(keys, query, ((1,), (1,)))
-            scores = jnp.where(mask, jnp.float32(-1e30), scores)
-            top = max_ref[head : head + 1, start:own]
-            inverse = inv_ref[head : head + 1, start:own]
-            probs = jnp.exp2((scores - top) * (scaling * LOG2E)) * inverse
-            prob_grad = dot(values, grad, ((1,), (1,)))
-            weighted = probs * prob_grad
-            row_delta = jnp.sum(weighted, 0, keepdims=True)
-            score_grad = (scaling * (weighted - probs * row_delta)).astype(jnp.bfloat16)
-            probs_low = probs.astype(jnp.bfloat16)
-            dq_t[lanes, start:own] = dot(keys, score_grad, ((0,), (0,)))
-            key_sum.append(dot(score_grad, query, ((1,), (0,))))
-            value_sum.append(dot(probs_low, grad, ((1,), (0,))))
-        for sum_list, own_ref, prompt_ref in (
-            (key_sum, dk_ref, dpk_ref),
-            (value_sum, dv_ref, dpv_ref),
-        ):
-            total = sum_list[-1]
-            for part in sum_list[:-1]:
-                count = part.shape[0]
-                total = jnp.concatenate([total[:count] + part, total[count:]], 0)
-            prompt_ref[:, lanes] = total[:pad].astype(jnp.bfloat16)
-            own_ref[:, lanes] = total[pad:].astype(jnp.bfloat16)
+    lanes = slice(head * head_size, (head + 1) * head_size)
+    key_sum, value_sum = [], []
+    for (start, size), mask in zip(parts, masks):
+        own = start + size
+        keys = jnp.concatenate([pk_ref[:, lanes], k_ref[:own, lanes]], 0)
+        values = jnp.concatenate([pv_ref[:, lanes], v_ref[:own, lanes]], 0)
+        query, grad = q_ref[start:own, lanes], g_ref[start:own, lanes]
+        scores = dot(keys, query, ((1,), (1,)))
+        scores = jnp.where(mask, jnp.float32(-1e30), scores)
+        top = max_ref[head : head + 1, start:own]
+        inverse = inv_ref[head : head + 1, start:own]
+        probs = jnp.exp2((scores - top) * (scaling * LOG2E)) * inverse
+        prob_grad = dot(values, grad, ((1,), (1,)))
+        weighted = probs * prob_grad
+        row_delta = jnp.sum(weighted, 0, keepdims=True)
+        score_grad = (scaling * (weighted - probs * row_delta)).astype(jnp.bfloat16)
+        probs_low = probs.astype(jnp.bfloat16)
+        dq_t[lanes, start:own] = dot(keys, score_grad, ((0,), (0,)))
+        key_sum.append(dot(score_grad, query, ((1,), (0,))))
+        value_sum.append(dot(probs_low, grad, ((1,), (0,))))
+    for sum_list, own_ref, prompt_ref in (
+        (key_sum, dk_ref, dpk_ref),
+        (value_sum, dv_ref, dpv_ref),
+    ):
+        total = sum_list[-1]
+        for part in sum_list[:-1]:
+            count = part.shape[0]
+            total = jnp.concatenate([total[:count] + part, total[count:]], 0)
+        prompt_ref[:, lanes] = total[:pad].astype(jnp.bfloat16)
+        own_ref[:, lanes] = total[pad:].astype(jnp.bfloat16)
+
+
+def bwd_kernel(sums, head_size, *refs):
+    dq_ref, dq_t = refs[8], refs[13]
+    for head in range(refs[0].shape[1] // head_size):
+        bwd_head(sums, head_size, head, refs[:8] + refs[9:])
     dq_ref[...] = dq_t[...].T.astype(jnp.bfloat16)
 
 
@@ -148,24 +138,26 @@
     )(query, key, value, prompt_k, prompt_v)
 
     plan = split_plan(n_seg, n_dp, width, out_grad.shape[1])
+    shapes = [low((tokens, width))] * 3 + [low((pad, width))] * 2
     if plan is None:
         weight_grad = plain_weight(attn_t, out_grad)
+        head_low = jnp.einsum("td,hd->th", out_grad, w_out, preferred_element_type=jnp.float32)
+        query_grad, key_grad, value_grad, pk_part, pv_part = pl.pallas_call(
+            functools.partial(bwd_kernel, sums, head_size),
+            grid=(HEADS // GROUP,),
+            in_specs=[own_spec] * 3 + [prompt_spec] * 2 + [own_spec, stat_spec, stat_spec],
+            out_specs=[own_spec] * 3 + [prompt_spec] * 2,
+            out_shape=shapes,
+            scratch_shapes=[pltpu.VMEM((group, tokens), jnp.float32)],
+            compiler_params=params,
+            cost_estimate=pl.CostEstimate(
+                flops=25 * flops, bytes_accessed=16 * tokens * width, transcendentals=0
+            ),
+        )(query, key, value, prompt_k, prompt_v, head_low.astype(jnp.bfloat16), top, inverse)
     else:
-        weight_grad = sum_weight(n_seg, n_dp, plan, attn_t, out_grad)
-
-    head_low = jnp.einsum("td,hd->th", out_grad, w_out, preferred_element_type=jnp.float32)
-    query_grad, key_grad, value_grad, pk_part, pv_part = pl.pallas_call(
-        functools.partial(bwd_kernel, sums, head_size),
-        grid=(HEADS // GROUP,),
-        in_specs=[own_spec] * 3 + [prompt_spec] * 2 + [own_spec, stat_spec, stat_spec],
-        out_specs=[own_spec] * 3 + [prompt_spec] * 2,
-        out_shape=[low((tokens, width))] * 3 + [low((pad, width))] * 2,
-        scratch_shapes=[pltpu.VMEM((group, tokens), jnp.float32)],
-        compiler_params=params,
-        cost_estimate=pl.CostEstimate(
-            flops=25 * flops, bytes_accessed=16 * tokens * width, transcendentals=0
-        ),
-    )(query, key, value, prompt_k, prompt_v, head_low.astype(jnp.bfloat16), top, inverse)
+        operands = (query, key, value, prompt_k, prompt_v, top, inverse)
+        outs = sum_weight(sums, head_size, plan, attn_t, out_grad, w_out, operands, shapes)
+        query_grad, key_grad, value_grad, pk_part, pv_part, weight_grad = outs
 
     parts = jnp.stack([pk_part, pv_part])
     segment = lax.axis_index("seg")
@@ -236,7 +228,12 @@
         body(pl.multiple_of(i * block, BLOCK), block)
 
 
-def sum_kernel(plans, attn_ref, grad_ref, out_ref, square_ref, acc, core_out, core_in, gath, square_out, square_in, *rest):
+def sum_kernel(plans, sums, head_size, *refs):
+    attn_ref, grad_ref, w_hbm = refs[:3]
+    own_refs, (max_ref, inv_ref) = refs[3:8], refs[8:10]
+    out_ref, square_ref, dq_ref, dk_ref, dv_ref, dpk_ref, dpv_ref = refs[10:17]
+    acc, core_out, core_in, gath, square_out, square_in, w_ref, g_ref, dq_t = refs[17:26]
+    rest = refs[26:]
     n_bits = len(plans[0])
     parts = len(plans)
     sends = [rest[p * n_bits : (p + 1) * n_bits] for p in range(parts)]
@@ -264,6 +261,25 @@
         copy.start()
         return copy
 
+    def head_grad(start, stop):
+        g_ref[:, start:stop] = dot(grad_ref[...], w_ref[start:stop, :], ((1,), (1,))).astype(
+            jnp.bfloat16
+        )
+
+    width = w_ref.shape[0]
+    chunk = 256 if width % 256 == 0 else width
+    chunks = [functools.partial(head_grad, at, at + chunk) for at in range(0, width, chunk)]
+    head_refs = own_refs + (g_ref, max_ref, inv_ref, dk_ref, dv_ref, dpk_ref, dpv_ref, dq_t)
+    heads = [
+        functools.partial(bwd_head, sums, head_size, head, head_refs) for head in range(HEADS)
+    ]
+    turns = [0]
+
+    def work():
+        turns[0] += 1
+        if turns[0] % 2 and heads:
+            heads.pop(0)()
+
     def part_rows(side, p):
         return pl.ds(pl.multiple_of(side * half + p * size, BLOCK), size)
 
@@ -279,6 +295,8 @@
     for device in [other] + partner:
         pl.semaphore_signal(barrier, inc=1, device_id=device, device_id_type=pl.DeviceIdType.MESH)
     pl.semaphore_wait(barrier, 1 + n_bits)
+    w_copy = pltpu.make_async_copy(w_hbm, w_ref, local_sem.at[2 * parts])
+    w_copy.start()
 
     core = []
     for p in range(parts):
@@ -309,6 +327,12 @@
             cast_given(acc, sends[p][stage], give, shape)
             flying[p] = send(sends[p][stage], recvs[p][stage], partner[b])
             history[p].append((b, keep, shape))
+            if stage > 0:
+                work()
+        if stage == 0:
+            w_copy.wait()
+            for piece in chunks:
+                piece()
 
     def gather(p, stage):
         b, keep, shape = history[p][stage]
@@ -323,6 +347,7 @@
         squares = squares + jnp.sum(own * own, keepdims=True)
         region(gath, (seg * half + keep[0], keep[1]), shape)[...] = own.astype(jnp.bfloat16)
         flying[p] = gather(p, n_bits - 1)
+        work()
     square_out[0] = jnp.broadcast_to(squares, square_out.shape[1:])
     square_copy = send(square_out.at[0], square_in.at[0], partner[0])
 
@@ -336,11 +361,15 @@
                 mine = gath.at[part_rows(seg, p), :]
                 flying[p] = send(mine, mine, other)
                 stores.append(store(seg, p))
+            work()
         step = n_bits - 1 - stage
         square_copy.wait()
         square_out[step + 1] = square_out[step] + square_in[step]
         device = partner[step + 1] if step + 1 < n_bits else other
         square_copy = send(square_out.at[step + 1], square_in.at[step + 1], device)
+    for head in heads:
+        head()
+    dq_ref[...] = dq_t[...].T.astype(jnp.bfloat16)
     square_copy.wait()
     square_ref[...] = square_out[n_bits] + square_in[n_bits]
     for p in range(parts):
@@ -370,7 +399,7 @@
     by_rows(shape[0], cast)
 
 
-def sum_weight(n_seg, n_dp, plans, attn_t, out_grad):
+def sum_weight(sums, head_size, plans, attn_t, out_grad, w_out, operands, grads):
     width, cols = attn_t.shape[0], out_grad.shape[1]
     half, bits, parts = width // 2, len(plans[0]), len(plans)
     low = functools.partial(pltpu.VMEM, dtype=jnp.bfloat16)
@@ -378,13 +407,16 @@
     buffers = [low(shape) for part in shapes for shape in part]
     copies = 2 * parts + 2 * parts * bits + bits + 1
     vmem = pl.BlockSpec(memory_space=pltpu.VMEM)
-    total, squares = pl.pallas_call(
-        functools.partial(sum_kernel, plans),
-        in_specs=[vmem] * 2,
-        out_specs=[pl.BlockSpec(memory_space=pl.ANY), vmem],
+    hbm = pl.BlockSpec(memory_space=pl.ANY)
+    tokens = out_grad.shape[0]
+    total, squares, *results = pl.pallas_call(
+        functools.partial(sum_kernel, plans, sums, head_size),
+        in_specs=[vmem] * 2 + [hbm] + [vmem] * len(operands),
+        out_specs=[hbm, vmem] + [vmem] * len(grads),
         out_shape=[
             jax.ShapeDtypeStruct((width, cols), jnp.bfloat16),
             jax.ShapeDtypeStruct((8, 128), jnp.float32),
+            *grads,
         ],
         scratch_shapes=[
             pltpu.VMEM((half, cols), jnp.float32),
@@ -393,23 +425,27 @@
             low((width, cols)),
             pltpu.VMEM((bits + 1, 8, 128), jnp.float32),
             pltpu.VMEM((bits + 1, 8, 128), jnp.float32),
+            low((width, cols)),
+            low((tokens, width)),
+            pltpu.VMEM((width, tokens), jnp.float32),
             *buffers,
             *buffers,
             pltpu.SemaphoreType.DMA((copies,)),
             pltpu.SemaphoreType.DMA((copies,)),
-            pltpu.SemaphoreType.DMA((2 * parts,)),
+            pltpu.SemaphoreType.DMA((2 * parts + 1,)),
         ],
         compiler_params=pltpu.CompilerParams(
-            collective_id=0, has_side_effects=True, vmem_limit_bytes=56 * 1024 * 1024
+            collective_id=0, has_side_effects=True, vmem_limit_bytes=60 * 1024 * 1024
         ),
         cost_estimate=pl.CostEstimate(
             flops=2 * width * cols * attn_t.shape[1],
             bytes_accessed=4 * width * cols,
             transcendentals=0,
         ),
-    )(attn_t, out_grad)
+    )(attn_t, out_grad, w_out, *operands)
     rms = jnp.sqrt(squares[0, 0] / (width * cols) + 1e-06)
-    return (total.astype(jnp.float32) * jnp.minimum(1.0, 1.0 / rms)).astype(jnp.bfloat16)
+    low_grad = (total.astype(jnp.float32) * jnp.minimum(1.0, 1.0 / rms)).astype(jnp.bfloat16)
+    return (*results, low_grad)
 
 
 def solution(mesh):

time: 149 us -> 135 us (0.906)
  Pallas kernels: 125 us -> 107 us
  local copies, waits for them, and re-layouts: 4.57 us -> 12.7 us
  matrix products: 6.58 us -> 0 us
    pallas_call x2 -> x1, Pallas kernels: 110 us -> 92.4 us  [sum_weight(): pl.pallas_call(functools.partial(sum_kernel, plans, sums, head_size), in_...]
    unnamed x14 -> x29, local copies, waits for them, and re-layouts: 2.4 us -> 10.6 us
    dot_general x1 -> x0, matrix products: 6.58 us -> none  [shards(): jnp.einsum('td,hd->th', out_grad, w_out, preferred_element_type=jnp.float32)]
  transfers between devices with their start and end apart: 1 -> 1, of which waited for: 0 -> 0; matrix products, arithmetic and copies ran while one was open for 5% -> 6% of each run, Pallas kernels for 61% -> 0%
where the time goes in v3:
time: 135 us; the launch traced here: 134 us
  Pallas kernels  107 us (79%)
  local copies, waits for them, and re-layouts  12.7 us (9%)
  other arithmetic  8.72 us (6%)
  blocking collectives  2.38 us (2%)
  between operations  1.49 us (1%)
    pallas_call x1, Pallas kernels, sum_weight(): pl.pallas_call(functools.partial(sum_kernel, plans, sums, head_size), in_...  92.4 us
    pallas_call x1, Pallas kernels, shards(): pl.pallas_call(functools.partial(fwd_kernel, sums, head_size), grid=(HEAD...  14.7 us
    unnamed x29, local copies, waits for them, and re-layouts  10.6 us
    convert_element_type x1, other arithmetic, sum_weight(): (total.astype(jnp.float32) * jnp.minimum(1.0, 1.0 / rms)).astype(jnp.bflo...  6.97 us
  transfers between devices with their start and end apart: 1, of which 0 were waited for; matrix products, arithmetic and copies ran while one was open for 6% of the time, Pallas kernels for 0%

profile of v3, /device:TPU:0, one launch (start us, length us, event | category | flops | bytes accessed | tf_op | source)
XLA Modules:
  0.0 133.8 jit_solution(3502646027710067936)
XLA Ops:
  0.6 1.1 copy.13
  1.7 0.0 copy-start.11
  1.8 1.1 copy.14
  2.9 0.6 pad_maximum_fusion
  3.5 0.0 copy-start
  3.5 0.0 copy-start.1
  3.5 2.4 %all_gather.3 = bf16[2,100,1280]{2,0,1:T(2,128)(2,1)S(1)} all-gather(bf16[2,50,1280]{2,0,1:T(2,128)(2,1)S(1)} %pad_maximum_fusion), channel_id=1, replica_groups=mesh['seg'=2,'dp'=16] {'seg'}, dimensions={1}, use_global_device_ids=true | all-gather | bytes 768000 | tf_op jit(solution)/shard_map/all_gather | solution.py:118
  5.9 0.2 slice.25
  6.1 0.0 copy-done.11
  6.1 0.1 copy_select_fusion
  6.2 0.0 copy-start.4
  6.3 0.0 copy-start.5
  6.3 0.0 copy-done
  6.3 0.0 copy-done.1
  6.3 0.0 copy-start.2
  6.3 1.4 %copy-done.2 = bf16[1,512,1280]{2,1,0:T(8,128)(2,1)S(1)} copy-done((bf16[1,512,1280]{2,1,0:T(8,128)(2,1)S(1)}, bf16[1,512,1280]{2,1,0:T(8,128)(2,1)}, u32[]{:S(2)}) %copy-start.2) | copy-done | bytes 1310744
  7.7 14.7 %shard_map.118 = (bf16[1280,512]{1,0:T(8,128)(2,1)S(1)}, f32[16,512]{1,0:T(8,128)S(1)}, f32[16,512]{1,0:T(8,128)S(1)}) custom-call(bf16[512,1280]{1,0:T(8,128)(2,1)S(1)} %bitcast.15, bf16[512,1280]{1,0:T(8,128)(2,1)S(1)} %bitcast.17, bf16[512,1280]{1,0:T(8,128)(2,1)S(1)} %bitcast.19, bf16[64,1280]{1,0:T(8,128)(2,1)S(1)} %get-tuple-element.27.pk_ref.refs_6_, ...), custom_call_target="tpu_custom_call" | custom-call | flops 6710886400 | bytes 5242880 | tf_op jit(solution)/shard_map/pallas_call | solution.py:128
  22.4 0.0 copy-done.4
  22.5 0.0 copy-done.5
  22.5 0.0 copy-start.3
  22.5 1.0 copy-done.3
  23.5 0.0 copy-start.6
  23.5 0.6 copy-done.6
  24.1 0.0 copy-start.7
  24.1 0.6 copy-done.7
  24.8 92.4 %shard_map.119 = (bf16[1280,2560]{1,0:T(8,128)(2,1)}, f32[8,128]{1,0:T(8,128)}, bf16[512,1280]{1,0:T(8,128)(2,1)}, bf16[512,1280]{1,0:T(8,128)(2,1)}, bf16[512,1...) custom-call(bf16[1280,512]{1,0:T(8,128)(2,1)} %copy-done.3, bf16[512,2560]{1,0:T(8,128)(2,1)} %bitcast.20, ...), custom_call_target="tpu_custom_call" | custom-call | flops 3355443200 | bytes 13107200 | tf_op jit(solution)/shard_map/pallas_call | solution.py:412
  117.2 1.1 fusion
  118.2 1.3 collective-permute-start
  119.5 1.2 slice.24
  121.4 0.0 copy-start.10
  121.4 7.0 %multiply_convert_fusion = bf16[1280,2560]{1,0:T(8,128)(2,1)} fusion(bf16[1280,2560]{1,0:T(8,128)(2,1)} %get-tuple-element.24, f32[]{:T(128)} %bitcast.11), kind=kLoop, calls=%fused_computation | loop fusion | flops 9830400 | bytes 13107204 | tf_op jit(solution)/shard_map/convert_element_type | solution.py:447
  128.4 0.0 collective-permute-done
  128.4 0.7 fusion.1
  129.1 0.0 copy-done.10
  129.1 0.0 copy-start.9
  129.1 1.1 copy.21
  130.2 0.7 copy-done.9
  130.9 0.0 copy-start.8
  130.9 1.1 copy.22
  132.0 0.7 copy-done.8
  132.7 1.1 copy.23
  (1 shorter events, 0.0 us)
Async XLA Ops:
  1.7 4.4 %copy-start.11 = (pred[64]{0:T(512)(128)(4,1)S(1)}, pred[64]{0:T(512)(128)(4,1)}, u32[]{:S(2)}) copy-start(pred[64]{0:T(512)(128)(4,1)} %constant.18.clone.1) | copy-start | bytes 196
  3.5 2.8 %copy-start = (bf16[1,512,1280]{2,1,0:T(8,128)(2,1)S(1)}, bf16[1,512,1280]{2,1,0:T(8,128)(2,1)}, u32[]{:S(2)}) copy-start(bf16[1,512,1280]{2,1,0:T(8,128)(2,1)} %param.7) | copy-start | bytes 3932164
  3.5 2.8 %copy-start.1 = (bf16[1,512,1280]{2,1,0:T(8,128)(2,1)S(1)}, bf16[1,512,1280]{2,1,0:T(8,128)(2,1)}, u32[]{:S(2)}) copy-start(bf16[1,512,1280]{2,1,0:T(8,128)(2,1)} %param.8) | copy-start | bytes 3932164
  6.2 16.2 %copy-start.4 = (bf16[64,1280]{1,0:T(8,128)(2,1)}, bf16[64,1280]{1,0:T(8,128)(2,1)S(1)}, u32[]{:S(2)}) copy-start(bf16[64,1280]{1,0:T(8,128)(2,1)S(1)} %get-tuple-element.26.pv_ref.refs_7_) | copy-start | bytes 491524
  6.3 16.2 %copy-start.5 = (bf16[64,1280]{1,0:T(8,128)(2,1)}, bf16[64,1280]{1,0:T(8,128)(2,1)S(1)}, u32[]{:S(2)}) copy-start(bf16[64,1280]{1,0:T(8,128)(2,1)S(1)} %get-tuple-element.27.pk_ref.refs_6_) | copy-start | bytes 491524
  6.3 1.4 %copy-start.2 = (bf16[1,512,1280]{2,1,0:T(8,128)(2,1)S(1)}, bf16[1,512,1280]{2,1,0:T(8,128)(2,1)}, u32[]{:S(2)}) copy-start(bf16[1,512,1280]{2,1,0:T(8,128)(2,1)} %param.9) | copy-start | bytes 3932164
  22.5 1.1 copy-start.3
  23.5 0.6 copy-start.6
  24.1 0.6 copy-start.7
  118.2 10.2 %collective-permute-start = (bf16[2,50,1280]{2,1,0:T(8,128)(2,1)S(1)}, bf16[2,50,1280]{2,1,0:T(8,128)(2,1)S(1)}, u32[]{:S(2)}, u32[]{:S(2)}) collective-permute-start(bf16[2,50,1280]{2,1,0:T(8,128)(2,1)S(1)} %fusion), channel_id=1, source_target_pairs={{16,0},{17,1},{18,2},{19,3},{20,4},{21,5},{22,6},{23,7},{24,8},{25... | collective-permute-start | bytes 768008 | tf_op jit(solution)/shard_map/ppermute | solution.py:169
  121.4 7.7 %copy-start.10 = (bf16[512,1280]{1,0:T(8,128)(2,1)S(1)}, bf16[512,1280]{1,0:T(8,128)(2,1)}, u32[]{:S(2)}) copy-start(bf16[512,1280]{1,0:T(8,128)(2,1)} %get-tuple-element.19) | copy-start | bytes 3932164
  129.1 1.8 %copy-start.9 = (bf16[512,1280]{1,0:T(8,128)(2,1)S(1)}, bf16[512,1280]{1,0:T(8,128)(2,1)}, u32[]{:S(2)}) copy-start(bf16[512,1280]{1,0:T(8,128)(2,1)} %get-tuple-element.20) | copy-start | bytes 3932164
  130.9 1.8 %copy-start.8 = (bf16[512,1280]{1,0:T(8,128)(2,1)S(1)}, bf16[512,1280]{1,0:T(8,128)(2,1)}, u32[]{:S(2)}) copy-start(bf16[512,1280]{1,0:T(8,128)(2,1)} %get-tuple-element.21) | copy-start | bytes 3932164
